TPU v7x, 256 devices: a whole 4x4x8 slice. The times are simulated.
256 devices in a mesh: gx: 16 (over z_hi, x), gy: 16 (over y, z_lo, core).
Axes of the slice: x: 4, y: 4, z: 8 (z_hi: 4, z_lo: 2; z = z_hi * 2 + z_lo), core: 2. Of those that a mesh axis runs over, the one named last changes fastest.
Arguments:
- field: bfloat16 [768, 128, 1536], P(None, 'gy', 'gx'), may hold values from -8 to 8
- norm_field: float32 [768, 128, 1536], P(('gx', 'gy')), may hold values from 0.5 to 2
- vertical: float32 [2, 64, 64], replicated, may hold values from -0.75 to 0.75
- x_filter: bfloat16 [1536, 1536], replicated, may hold values from -2 to 2
- y_filter: bfloat16 [768, 768], replicated, may hold values from -2 to 2
Outputs:
- covaried: bfloat16 [768, 128, 1536], P(None, 'gy', 'gx')
All inputs are finite; a program needn't handle non-finite values.
Results may differ from a plain program's by a relative error of at most 0.0075.
Values may be sent and summed in bfloat16 or wider, within the bound.
No kernel may reach another device: no remote copies, remote signals or barrier semaphores. Data moves between devices by JAX's collectives and lax.ppermute only.
A program may use at most 64 MiB of HBM per device.

v0:
```python
import jax
import jax.numpy as jnp
from jax import lax
from jax.sharding import PartitionSpec as P


def xlines_forward(block, x_filter):
    width = x_filter.shape[0]
    result = jnp.dot(block.reshape(-1, width), x_filter, preferred_element_type=jnp.float32)
    return result.astype(jnp.bfloat16).reshape(block.shape)


def xlines_adjoint(block, x_filter):
    width = x_filter.shape[0]
    result = lax.dot_general(
        block.reshape(-1, width),
        x_filter,
        (((1,), (1,)), ((), ())),
        preferred_element_type=jnp.float32,
    )
    return result.astype(jnp.bfloat16).reshape(block.shape)


def columns_work(block, scales, vertical):
    species = vertical.shape[0]
    levels = vertical.shape[1]
    rows, comps, width = block.shape
    scaled = (scales * block.astype(jnp.float32)).reshape(rows, species, levels, width)
    lowered = jnp.einsum("slk,rslx->rskx", vertical, scaled, precision=lax.Precision.HIGHEST)
    raised = jnp.einsum("skl,rslx->rskx", vertical, lowered, precision=lax.Precision.HIGHEST)
    return (scales * raised.reshape(rows, comps, width)).astype(jnp.bfloat16)


def per_device(field, norm_field, vertical, x_filter, y_filter):
    lines, comps, width = field.shape
    first = lax.dot_general(
        y_filter,
        field.reshape(lines, comps * width),
        (((0,), (0,)), ((), ())),
        preferred_element_type=jnp.float32,
    )
    first = first.astype(jnp.bfloat16).reshape(lines, comps, width)
    xblock = lax.all_to_all(first, "gx", split_axis=0, concat_axis=2, tiled=True)
    second = xlines_forward(xblock, x_filter)
    columns = lax.all_to_all(second, "gy", split_axis=0, concat_axis=1, tiled=True)
    middle = columns_work(columns, norm_field, vertical)
    returned = lax.all_to_all(middle, "gy", split_axis=1, concat_axis=0, tiled=True)
    third = xlines_adjoint(returned, x_filter)
    ylines = lax.all_to_all(third, "gx", split_axis=2, concat_axis=0, tiled=True)
    result = jnp.dot(
        y_filter, ylines.reshape(lines, comps * width), preferred_element_type=jnp.float32
    )
    return result.astype(jnp.bfloat16).reshape(lines, comps, width)


def solution(mesh):
    return jax.shard_map(
        per_device,
        mesh=mesh,
        in_specs=(P(None, "gy", "gx"), P(("gx", "gy"), None, None), P(), P(), P()),
        out_specs=P(None, "gy", "gx"),
        check_vma=False,
    )
```

profile of v0, /device:TPU:32, one launch (start us, length us, event | category | flops | bytes accessed | tf_op | source)
XLA Modules:
  0.0 183.3 jit_solution(692542181983948641)
XLA Ops:
  0.0 0.0 copy-start
  0.0 1.3 copy-done
  1.3 3.4 %convolution_convert_fusion.2 = bf16[768,768]{0,1:T(8,128)(2,1)} fusion(bf16[768,768]{0,1:T(8,128)(2,1)S(1)} %bitcast.62, bf16[768,768]{1,0:T(8,128)(2,1)} %param.9), kind=kOutput, calls=%fused_computation.10 | convolution fusion | flops 906559488 | bytes 3538944 | tf_op jit(solution)/shard_map/dot_general | solution.py:36
  4.6 2.1 %copy.42 = bf16[768,8,96]{2,1,0:T(8,128)(2,1)S(1)} copy(bf16[768,8,96]{0,2,1:T(8,128)(2,1)} %bitcast.70) | data formatting | bytes 2359296 | tf_op jit(solution)/shard_map/reshape | solution.py:42
  6.7 50.6 %all_to_all.54 = bf16[768,8,96]{2,1,0:T(8,128)(2,1)S(1)} all-to-all(bf16[768,8,96]{2,1,0:T(8,128)(2,1)S(1)} %copy.42), channel_id=1, replica_groups=mesh['gx'=16,'gy'=16] {'gx'}, dimensions={0} | all-to-all | bytes 2359296 | tf_op jit(solution)/shard_map/all_to_all | solution.py:43
  57.4 1.8 copy.43
  59.2 2.7 %reshape.39 = bf16[384,1536]{1,0:T(8,128)(2,1)} reshape(bf16[48,8,16,96]{3,2,1,0:T(8,128)(2,1)S(1)} %copy.43) | data formatting | bytes 2359296 | tf_op jit(solution)/shard_map/reshape | solution.py:9
  61.9 4.7 %fusion = bf16[48,8,1536]{2,1,0:T(8,128)(2,1)S(1)} fusion(bf16[384,1536]{1,0:T(8,128)(2,1)} %reshape.39, bf16[1536,1536]{1,0:T(8,128)(2,1)} %param.8), kind=kOutput, calls=%fused_computation.4 | convolution fusion | flops 1812529152 | bytes 7077888 | tf_op jit(solution)/shard_map/dot_general | solution.py:9
  66.5 0.0 copy-start.1
  66.6 22.6 %all_to_all.55 = bf16[48,8,1536]{2,1,0:T(8,128)(2,1)S(1)} all-to-all(bf16[48,8,1536]{2,1,0:T(8,128)(2,1)S(1)} %fusion), channel_id=1, replica_groups=mesh['gx'=16,'gy'=16] {'gy'}, dimensions={0} | all-to-all | bytes 2359296 | tf_op jit(solution)/shard_map/all_to_all | solution.py:45
  89.2 0.0 copy-done.1
  89.2 0.0 copy-start.2
  89.2 0.4 bitcast_multiply_fusion
  89.6 0.5 copy-done.2
  90.0 2.2 %convolution_bitcast_fusion.1 = f32[3,2,64,1536]{3,2,0,1:T(8,128)S(1)} fusion(f32[3,2,64,1536]{3,2,1,0:T(8,128)S(1)} %bitcast.65, f32[2,64,64]{2,1,0:T(8,128)S(1)} %copy-done.2), kind=kOutput, calls=%fused_computation.1 | convolution fusion | flops 452984832 | bytes 4751360 | tf_op jit(solution)/shard_map/slk,rslx->rskx/dot_general | solution.py:29
  92.3 2.3 %convolution_bitcast_fusion = f32[3,2,64,1536]{3,2,0,1:T(8,128)S(1)} fusion(f32[3,2,64,1536]{3,2,0,1:T(8,128)S(1)} %convolution_bitcast_fusion.1, f32[2,64,64]{2,1,0:T(8,128)S(1)} %copy-done.2), kind=kOutput, calls=%fused_computation | convolution fusion | flops 452984832 | bytes 4751360 | tf_op jit(solution)/shard_map/skl,rslx->rskx/dot_general | solution.py:30
  94.6 0.2 copy.47
  94.8 0.4 fusion.2
  95.3 0.0 slice-start
  95.3 1.0 copy.48
  96.3 0.0 slice-start.1
  96.3 24.9 %all_to_all.56 = bf16[3,128,1536]{2,0,1:T(4,128)(2,1)S(1)} all-to-all(bf16[3,128,1536]{2,0,1:T(4,128)(2,1)S(1)} %copy.48), channel_id=1, replica_groups=mesh['gx'=16,'gy'=16] {'gy'}, dimensions={1} | all-to-all | bytes 2359296 | tf_op jit(solution)/shard_map/all_to_all | solution.py:47
  121.2 0.2 copy.64
  121.5 0.1 copy.50
  121.5 0.0 slice-done
  121.6 0.0 slice-done.1
  121.6 2.0 %fusion.1 = bf16[48,8,1536]{2,1,0:T(8,128)(2,1)S(1)} fusion(bf16[384,1536]{1,0:T(8,128)(2,1)S(1)} %bitcast.69, bf16[1536,1536]{1,0:T(8,128)(2,1)S(1)} %bitcast.72), kind=kOutput, calls=%fused_computation.5 | convolution fusion | flops 1812529152 | bytes 7077888 | tf_op jit(solution)/shard_map/dot_general | solution.py:15
  123.6 3.8 %copy.51 = bf16[48,8,1536]{0,1,2:T(8,128)(2,1)} copy(bf16[48,8,1536]{2,1,0:T(8,128)(2,1)S(1)} %fusion.1) | data formatting | bytes 2359296 | tf_op jit(solution)/shard_map/reshape | solution.py:21
  127.4 5.7 %reshape.51 = bf16[16,2,18432]{2,1,0:T(2,128)(2,1)S(1)} reshape(bf16[1536,8,48]{2,1,0:T(8,128)(2,1)} %bitcast.64) | data formatting | bytes 2359296
  133.1 36.2 %all_to_all.57 = bf16[16,2,18432]{2,1,0:T(2,128)(2,1)S(1)} all-to-all(bf16[16,2,18432]{2,1,0:T(2,128)(2,1)S(1)} %reshape.51), channel_id=1, replica_groups=mesh['gx'=16,'gy'=16] {'gx'}, dimensions={0} | all-to-all | bytes 2359296 | tf_op jit(solution)/shard_map/all_to_all | solution.py:49
  169.3 4.1 %reshape.52 = bf16[1536,8,48]{2,1,0:T(8,128)(2,1)} reshape(bf16[16,2,18432]{2,1,0:T(2,128)(2,1)S(1)} %all_to_all.57) | data formatting | bytes 2359296
  173.4 4.0 %copy.53 = bf16[16,48,8,96]{3,2,1,0:T(8,128)(2,1)S(1)} copy(bf16[16,48,8,96]{1,2,3,0:T(8,128)(2,1)} %bitcast.63) | data formatting | bytes 2359296 | tf_op jit(solution)/shard_map/all_to_all | solution.py:49
  177.4 2.2 %reshape.45 = bf16[768,768]{1,0:T(8,128)(2,1)} reshape(bf16[16,48,8,96]{3,2,1,0:T(8,128)(2,1)S(1)} %copy.53) | data formatting | bytes 2359296 | tf_op jit(solution)/shard_map/reshape | solution.py:51
  179.5 3.8 %convolution_convert_fusion.3 = bf16[768,768]{1,0:T(8,128)(2,1)} fusion(bf16[768,768]{1,0:T(8,128)(2,1)} %reshape.45, bf16[768,768]{1,0:T(8,128)(2,1)} %param.9), kind=kOutput, calls=%fused_computation.11 | convolution fusion | flops 906559488 | bytes 3538944 | tf_op jit(solution)/shard_map/dot_general | solution.py:50
  (1 shorter events, 0.0 us)
Async XLA Ops:
  0.0 1.3 copy-start
  66.5 22.6 %copy-start.1 = (f32[3,128,1536]{2,1,0:T(8,128)S(1)}, f32[3,128,1536]{2,1,0:T(8,128)}, u32[]{:S(2)}) copy-start(f32[3,128,1536]{2,1,0:T(8,128)} %param.6) | copy-start | bytes 7077892
  89.2 0.8 copy-start.2
  95.3 26.3 %slice-start = ((s8[4718592]{0:T(1024)(128)(4,1)}), s8[4194304]{0:T(1024)(128)(4,1)S(1)}, s32[]{:S(2)}) async-start(s8[4718592]{0:T(1024)(128)(4,1)} %bitcast.71), calls=%async_computation.4 | async-start | bytes 8388608
  96.3 25.2 %slice-start.1 = ((s8[4718592]{0:T(1024)(128)(4,1)}), s8[524288]{0:T(1024)(128)(4,1)S(1)}, s32[]{:S(2)}) async-start(s8[4718592]{0:T(1024)(128)(4,1)} %bitcast.71), calls=%async_computation.5 | async-start | bytes 1048576
where the time goes:
time: 184 us; the launch traced here: 183 us
  blocking collectives  134 us (73%)
  local copies, waits for them, and re-layouts  29.7 us (16%)
  matrix products  18.4 us (10%)
    all_to_all x1, blocking collectives, per_device(): lax.all_to_all(first, 'gx', split_axis=0, concat_axis=2, tiled=True)  50.6 us
    all_to_all x1, blocking collectives, per_device(): lax.all_to_all(third, 'gx', split_axis=2, concat_axis=0, tiled=True)  36.2 us
    all_to_all x1, blocking collectives, per_device(): lax.all_to_all(middle, 'gy', split_axis=1, concat_axis=0, tiled=True)  24.9 us
    all_to_all x1, blocking collectives, per_device(): lax.all_to_all(second, 'gy', split_axis=0, concat_axis=1, tiled=True)  22.6 us
    unnamed x12, local copies, waits for them, and re-layouts  11.5 us
    dot_general x1, matrix products, xlines_forward(): jnp.dot(block.reshape(-1, width), x_filter, preferred_element_type=jnp.fl...  4.69 us
    all_to_all x1, local copies, waits for them, and re-layouts, per_device(): lax.all_to_all(third, 'gx', split_axis=2, concat_axis=0, tiled=True)  4 us
    reshape x1, local copies, waits for them, and re-layouts, xlines_adjoint(): return result.astype(jnp.bfloat16).reshape(block.shape)  3.82 us

commit v1 on v0

v1 whole, which is shorter than its diff:
```python
import functools

import jax
import jax.numpy as jnp
import numpy as np
from jax import lax
from jax.experimental import pallas as pl
from jax.experimental.pallas import tpu as pltpu
from jax.sharding import PartitionSpec as P

LANES = 128
WIDTH = 96
PIECE = 32
MAIN = 6
ROWS = 3
COMPS = 8
MESSAGE = ROWS * MAIN
F32 = jnp.float32
BF16 = jnp.bfloat16


def dot(a, b, contract):
    return lax.dot_general(a, b, ((contract[:1], contract[1:]), ((), ())), preferred_element_type=F32)


def spread_kernel(field_ref, filter_ref, out_ref, rows_ref):
    filt = filter_ref[...]
    lines = filt.shape[0]
    for pair in range(MAIN // 2):
        parts = []
        for j in (2 * pair, 2 * pair + 1):
            start = PIECE * (j % 3)
            parts += [field_ref[j], field_ref[MAIN + j // 3, start : start + PIECE, :]]
        first = dot(filt, jnp.concatenate(parts, axis=0), (0, 1))
        for half in range(2):
            rows_ref[pl.ds(2 * pair + half, lines, stride=MAIN), :] = first[:, half * LANES : (half + 1) * LANES]
    out_ref[...] = rows_ref[...].astype(BF16)


def gather_kernel(rows_in_ref, filter_ref, out_ref, rows_ref):
    filt = filter_ref[...]
    lines = filt.shape[0]
    rows_ref[...] = rows_in_ref[...].astype(F32)
    for j in range(MAIN):
        third = rows_ref[pl.ds(j, lines, stride=MAIN), :].astype(BF16)
        unit = (
            lax.broadcasted_iota(jnp.int32, (LANES, LANES), 0) == lax.broadcasted_iota(jnp.int32, (LANES, LANES), 1)
        ).astype(BF16)
        turned = dot(unit, third, (1, 1)).astype(BF16)
        result = dot(turned, filt, (1, 1)).astype(BF16)
        start = PIECE * (j % 3)
        out_ref[j] = result[:WIDTH]
        out_ref[MAIN + j // 3, start : start + PIECE, :] = result[WIDTH:]


def middle_kernel(rows_in_ref, filter_ref, norm_ref, vertical_ref, order_ref, out_ref, rows_ref, tail_ref, *, tiles, owners):
    filt = filter_ref[...]
    order = order_ref[...]
    block = owners * MESSAGE
    rest = block // 3
    rows_ref[...] = rows_in_ref[...].astype(F32)
    main = [rows_ref[block * g : block * (g + 1), :WIDTH] for g in range(tiles)]
    left = jnp.concatenate(main, axis=1).astype(BF16)
    tail = []
    for g in range(tiles):
        for t in range(3):
            tail.append(rows_ref[pl.ds(block * g + t, rest, stride=3), :][:, WIDTH:])
    below = jnp.concatenate(tail, axis=1).astype(BF16)
    lines = jnp.concatenate([left, below], axis=0)
    second = dot(lines, filt, (1, 0)).astype(BF16)
    second = dot(order, second, (1, 0))
    comps = norm_ref.shape[1]
    levels = vertical_ref.shape[1]
    raised = []
    for r in range(ROWS):
        for s in range(vertical_ref.shape[0]):
            factor = vertical_ref[s]
            weight = lax.dot_general(
                factor, factor, (((1,), (1,)), ((), ())), precision=lax.Precision.HIGHEST, preferred_element_type=F32
            )
            high = weight.astype(BF16)
            low = (weight - high.astype(F32)).astype(BF16)
            span = slice(s * levels, (s + 1) * levels)
            scales = norm_ref[r, span, :]
            scaled = scales * second[r * comps + s * levels : r * comps + (s + 1) * levels]
            upper = scaled.astype(BF16)
            under = (scaled - upper.astype(F32)).astype(BF16)
            product = dot(
                jnp.concatenate([high, high, low], axis=1), jnp.concatenate([upper, under, upper], axis=0), (1, 0)
            )
            raised.append((scales * product).astype(BF16))
    middle = jnp.concatenate(raised, axis=0)
    middle = dot(order, middle, (0, 0)).astype(BF16)
    third = dot(middle, filt, (1, 1))
    lane = lax.broadcasted_iota(jnp.int32, (block, LANES), 1)
    for g in range(tiles):
        start = WIDTH * g
        for t in range(3):
            at = start + PIECE * t
            tile = third[block:, at - at % LANES : at - at % LANES + LANES]
            tail_ref[pl.ds(t, rest, stride=3), :] = pltpu.roll(tile, (WIDTH - at) % LANES, 1)
        piece = third[:block, start : start + WIDTH]
        piece = jnp.concatenate([piece, jnp.zeros((block, PIECE), F32)], axis=1)
        out_ref[block * g : block * (g + 1), :] = jnp.where(lane < WIDTH, piece, tail_ref[...]).astype(BF16)


def arrival_order(owners):
    block = owners * MESSAGE
    comps = owners * COMPS
    table = np.zeros((ROWS * comps, ROWS * comps), np.float32)
    for owner in range(owners):
        for row in range(ROWS):
            for j in range(MAIN):
                table[row * comps + owner * COMPS + j, owner * MESSAGE + row * MAIN + j] = 1
            for i in range(2):
                table[row * comps + owner * COMPS + MAIN + i, block + owner * MAIN + row * 2 + i] = 1
    return table


def in_vmem(count):
    return [pl.BlockSpec(memory_space=pltpu.VMEM)] * count


def per_device(tiles, owners, field, norm_field, vertical, x_filter, y_filter):
    lines, comps, width = field.shape
    total = tiles * owners * MESSAGE
    params = pltpu.CompilerParams(vmem_limit_bytes=40 * 1024 * 1024)
    message_rows = jax.ShapeDtypeStruct((total, LANES), BF16)
    rows_scratch = pltpu.VMEM((total, LANES), F32)

    def exchange(rows):
        grouped = rows.reshape(tiles * owners, MESSAGE // 2, 2, LANES)
        moved = lax.all_to_all(grouped, ("gx", "gy"), split_axis=0, concat_axis=0, tiled=True)
        return moved.reshape(total, LANES)

    rows = pl.pallas_call(
        spread_kernel,
        out_shape=message_rows,
        in_specs=in_vmem(2),
        out_specs=pl.BlockSpec(memory_space=pltpu.VMEM),
        scratch_shapes=[rows_scratch],
        compiler_params=params,
        name="spread",
    )(jnp.transpose(field, (1, 2, 0)), y_filter)
    rows = exchange(rows)
    rows = pl.pallas_call(
        functools.partial(middle_kernel, tiles=tiles, owners=owners),
        out_shape=message_rows,
        in_specs=in_vmem(5),
        out_specs=pl.BlockSpec(memory_space=pltpu.VMEM),
        scratch_shapes=[rows_scratch, pltpu.VMEM((owners * MESSAGE, LANES), F32)],
        compiler_params=params,
        name="middle",
    )(rows, x_filter, norm_field, vertical, jnp.asarray(arrival_order(owners), BF16))
    rows = exchange(rows)
    result = pl.pallas_call(
        gather_kernel,
        out_shape=jax.ShapeDtypeStruct((comps, width, lines), BF16),
        in_specs=in_vmem(2),
        out_specs=pl.BlockSpec(memory_space=pltpu.VMEM),
        scratch_shapes=[rows_scratch],
        compiler_params=params,
        name="gather",
    )(rows, y_filter)
    return jnp.transpose(result, (2, 0, 1))


def solution(mesh):
    return jax.shard_map(
        functools.partial(per_device, mesh.shape["gx"], mesh.shape["gy"]),
        mesh=mesh,
        in_specs=(P(None, "gy", "gx"), P(("gx", "gy"), None, None), P(), P(), P()),
        out_specs=P(None, "gy", "gx"),
        check_vma=False,
    )
```

time: 184 us -> 107 us (0.58)
  the two profiles are of different devices: /device:TPU:32 before, /device:TPU:1 now
where the time goes in v1:
time: 107 us; the launch traced here: 106 us
  blocking collectives  90.4 us (84%)
  Pallas kernels  11.7 us (11%)
  local copies, waits for them, and re-layouts  4.22 us (4%)
    all_to_all x2, blocking collectives, exchange(): lax.all_to_all(grouped, ('gx', 'gy'), split_axis=0, concat_axis=0, tiled=...  90.4 us
    pallas_call x1, Pallas kernels, per_device(): pl.pallas_call(functools.partial(middle_kernel, tiles=tiles, owners=owner...  6.81 us
    unnamed x14, local copies, waits for them, and re-layouts  4.22 us
    pallas_call x1, Pallas kernels, per_device(): pl.pallas_call(gather_kernel, out_shape=jax.ShapeDtypeStruct((comps, widt...  3.71 us

profile of v1, /device:TPU:1, one launch (start us, length us, event | category | flops | bytes accessed | tf_op | source)
XLA Modules:
  0.0 106.4 jit_solution(12779934172487318632)
XLA Ops:
  0.0 0.0 copy-start
  0.0 1.3 %copy-done = bf16[768,768]{1,0:T(8,128)(2,1)S(1)} copy-done((bf16[768,768]{1,0:T(8,128)(2,1)S(1)}, bf16[768,768]{1,0:T(8,128)(2,1)}, u32[]{:S(2)}) %copy-start) | copy-done | bytes 1179672
  1.3 0.0 copy-start.4
  1.3 1.3 %copy-done.4 = bf16[768,8,96]{0,2,1:T(8,128)(2,1)S(1)} copy-done((bf16[768,8,96]{0,2,1:T(8,128)(2,1)S(1)}, bf16[768,8,96]{0,2,1:T(8,128)(2,1)}, u32[]{:S(2)}) %copy-start.4) | copy-done | bytes 1179672
  2.5 0.0 copy-start.2
  2.5 1.2 %spread.1 = bf16[4608,128]{1,0:T(8,128)(2,1)S(1)} custom-call(bf16[8,96,768]{2,1,0:T(8,128)(2,1)S(1)} %bitcast.10, bf16[768,768]{1,0:T(8,128)(2,1)S(1)} %copy-done), custom_call_target="tpu_custom_call" | custom-call | tf_op jit(solution)/shard_map/spread/pallas_call | solution.py:136
  3.8 0.0 copy-start.5
  3.8 0.0 copy-start.6
  3.8 50.7 %all_to_all.10 = bf16[256,9,2,128]{3,2,1,0:T(2,128)(2,1)S(1)} all-to-all(bf16[256,9,2,128]{3,2,1,0:T(2,128)(2,1)S(1)} %bitcast.9), channel_id=1, replica_groups=mesh['gx'=16,'gy'=16] {'gx','gy'}, dimensions={0} | all-to-all | bytes 2359296 | tf_op jit(solution)/shard_map/all_to_all | solution.py:133
  54.5 0.0 copy-done.2
  54.5 0.0 copy-done.5
  54.5 0.0 copy-done.6
  54.5 0.0 copy-start.3
  54.5 1.7 %copy-done.3 = f32[3,128,1536]{2,1,0:T(8,128)S(1)} copy-done((f32[3,128,1536]{2,1,0:T(8,128)S(1)}, f32[3,128,1536]{2,1,0:T(8,128)}, u32[]{:S(2)}) %copy-start.3) | copy-done | bytes 2359320
  56.1 6.8 %middle.1 = bf16[4608,128]{1,0:T(8,128)(2,1)S(1)} custom-call(bf16[4608,128]{1,0:T(8,128)(2,1)S(1)} %bitcast.6, bf16[1536,1536]{1,0:T(8,128)(2,1)S(1)} %copy-done.2, f32[3,128,1536]{2,1,0:T(8,128)S(1)} %copy-done.3, f32[2,64,64]{2,1,0:T(8,128)S(1)} %copy-done.6, bf16[384,384]{1,0:T(8,128)(2,1)S(1)} %copy-done.5), custom_call_target="tpu_custom_call" | custom-call | tf_op jit(solution)/shard_map/middle/pallas_call | solution.py:146
  63.0 0.0 copy-start.1
  63.0 39.8 %all_to_all.11 = bf16[256,9,2,128]{3,2,1,0:T(2,128)(2,1)S(1)} all-to-all(bf16[256,9,2,128]{3,2,1,0:T(2,128)(2,1)S(1)} %bitcast.7), channel_id=1, replica_groups=mesh['gx'=16,'gy'=16] {'gx','gy'}, dimensions={0} | all-to-all | bytes 2359296 | tf_op jit(solution)/shard_map/all_to_all | solution.py:133
  102.7 0.0 copy-done.1
  102.7 3.7 %gather.1 = bf16[8,96,768]{2,1,0:T(8,128)(2,1)} custom-call(bf16[4608,128]{1,0:T(8,128)(2,1)S(1)} %bitcast.8, bf16[768,768]{1,0:T(8,128)(2,1)S(1)} %copy-done.1), custom_call_target="tpu_custom_call" | custom-call | tf_op jit(solution)/shard_map/gather/pallas_call | solution.py:156
Async XLA Ops:
  0.0 1.3 %copy-start = (bf16[768,768]{1,0:T(8,128)(2,1)S(1)}, bf16[768,768]{1,0:T(8,128)(2,1)}, u32[]{:S(2)}) copy-start(bf16[768,768]{1,0:T(8,128)(2,1)} %filter_ref.5) | copy-start | bytes 3538948
  1.3 1.3 %copy-start.4 = (bf16[768,8,96]{0,2,1:T(8,128)(2,1)S(1)}, bf16[768,8,96]{0,2,1:T(8,128)(2,1)}, u32[]{:S(2)}) copy-start(bf16[768,8,96]{0,2,1:T(8,128)(2,1)} %param.6) | copy-start | bytes 3538948
  2.5 51.9 %copy-start.2 = (bf16[1536,1536]{1,0:T(8,128)(2,1)S(1)}, bf16[1536,1536]{1,0:T(8,128)(2,1)}, u32[]{:S(2)}) copy-start(bf16[1536,1536]{1,0:T(8,128)(2,1)} %filter_ref.4) | copy-start | bytes 14155780
  3.8 50.7 %copy-start.5 = (bf16[384,384]{1,0:T(8,128)(2,1)S(1)}, bf16[384,384]{1,0:T(8,128)(2,1)}, u32[]{:S(2)}) copy-start(bf16[384,384]{1,0:T(8,128)(2,1)} %constant.2.clone.order_ref) | copy-start | bytes 884740
  3.8 50.7 %copy-start.6 = (f32[2,64,64]{2,1,0:T(8,128)S(1)}, f32[2,64,64]{2,1,0:T(8,128)}, u32[]{:S(2)}) copy-start(f32[2,64,64]{2,1,0:T(8,128)} %vertical_ref.1) | copy-start | bytes 98308
  54.5 1.7 %copy-start.3 = (f32[3,128,1536]{2,1,0:T(8,128)S(1)}, f32[3,128,1536]{2,1,0:T(8,128)}, u32[]{:S(2)}) copy-start(f32[3,128,1536]{2,1,0:T(8,128)} %norm_ref.1) | copy-start | bytes 7077892
  63.0 39.8 %copy-start.1 = (bf16[768,768]{1,0:T(8,128)(2,1)S(1)}, bf16[768,768]{1,0:T(8,128)(2,1)}, u32[]{:S(2)}) copy-start(bf16[768,768]{1,0:T(8,128)(2,1)} %filter_ref.5) | copy-start | bytes 3538948

commit v2 on v1

v2 whole, which is shorter than its diff:
```python
import functools

import jax
import jax.numpy as jnp
import numpy as np
from jax import lax
from jax.experimental import pallas as pl
from jax.experimental.pallas import tpu as pltpu
from jax.sharding import PartitionSpec as P

LANES = 128
WIDTH = 96
PIECE = 32
MAIN = 6
ROWS = 3
COMPS = 8
MESSAGE = ROWS * MAIN
F32 = jnp.float32
BF16 = jnp.bfloat16


def dot(a, b, contract):
    return lax.dot_general(a, b, ((contract[:1], contract[1:]), ((), ())), preferred_element_type=F32)


def spread_kernel(field_ref, filter_ref, out_ref, rows_ref):
    lines = filter_ref.shape[0]
    parts = []
    for j in range(MAIN):
        start = PIECE * (j % 3)
        parts += [field_ref[j], field_ref[MAIN + j // 3, start : start + PIECE, :]]
    lines_in = jnp.concatenate(parts, axis=0)
    chunk = lines // 3
    for at in range(0, lines, chunk):
        first = dot(filter_ref[:, at : at + chunk], lines_in, (0, 1))
        for j in range(MAIN):
            rows_ref[pl.ds(MAIN * at + j, chunk, stride=MAIN), :] = first[:, j * LANES : (j + 1) * LANES]
        span = pl.ds(MAIN * at, MAIN * chunk)
        out_ref[span, :] = rows_ref[span, :].astype(BF16)


def gather_kernel(rows_in_ref, filter_ref, out_hbm, rows_ref, out_ref, sems):
    filt = filter_ref[...]
    lines = filt.shape[0]
    rows_ref[...] = rows_in_ref[...].astype(F32)
    stores = []
    for side in range(2):
        turned = []
        for j in range(3 * side, 3 * side + 3):
            turned.append(jnp.transpose(rows_ref[pl.ds(j, lines, stride=MAIN), :].astype(BF16)))
        result = dot(jnp.concatenate(turned, axis=0), filt, (1, 1)).astype(BF16)
        for t in range(3):
            out_ref[3 * side + t] = result[LANES * t : LANES * t + WIDTH]
            out_ref[MAIN + side, PIECE * t : PIECE * (t + 1), :] = result[LANES * t + WIDTH : LANES * (t + 1)]
        for n, span in enumerate((pl.ds(3 * side, 3), pl.ds(MAIN + side, 1))):
            stores.append(pltpu.make_async_copy(out_ref.at[span], out_hbm.at[span], sems.at[2 * side + n]))
            stores[-1].start()
    for store in stores:
        store.wait()


def middle_kernel(
    rows_in_ref, filter_ref, norm_ref, vertical_ref, order_ref, out_ref, rows_ref, tail_ref, *, tiles, owners
):
    weights = []
    for s in range(vertical_ref.shape[0]):
        factor = vertical_ref[s]
        weight = lax.dot_general(
            factor, factor, (((1,), (1,)), ((), ())), precision=lax.Precision.HIGHEST, preferred_element_type=F32
        )
        high = weight.astype(BF16)
        low = (weight - high.astype(F32)).astype(BF16)
        weights.append(jnp.concatenate([high, high, low], axis=1))
    filt = filter_ref[...]
    order = order_ref[...]
    block = owners * MESSAGE
    rest = block // 3
    rows_ref[...] = rows_in_ref[...].astype(F32)
    main = [rows_ref[block * g : block * (g + 1), :WIDTH] for g in range(tiles)]
    left = jnp.concatenate(main, axis=1).astype(BF16)
    tail = []
    for g in range(tiles):
        for t in range(3):
            tail.append(rows_ref[pl.ds(block * g + t, rest, stride=3), :][:, WIDTH:])
    below = jnp.concatenate(tail, axis=1).astype(BF16)
    lines = jnp.concatenate([left, below], axis=0)
    second = dot(lines, filt, (1, 0)).astype(BF16)
    second = dot(order, second, (1, 0))
    comps = norm_ref.shape[1]
    levels = vertical_ref.shape[1]
    raised = []
    for r in range(ROWS):
        for s in range(vertical_ref.shape[0]):
            span = slice(s * levels, (s + 1) * levels)
            scales = norm_ref[r, span, :]
            scaled = scales * second[r * comps + s * levels : r * comps + (s + 1) * levels]
            upper = scaled.astype(BF16)
            under = (scaled - upper.astype(F32)).astype(BF16)
            product = dot(weights[s], jnp.concatenate([upper, under, upper], axis=0), (1, 0))
            raised.append((scales * product).astype(BF16))
    middle = jnp.concatenate(raised, axis=0)
    middle = dot(order, middle, (0, 0)).astype(BF16)
    third = dot(middle, filt, (1, 1))
    lane = lax.broadcasted_iota(jnp.int32, (block, LANES), 1)
    for g in range(tiles):
        start = WIDTH * g
        for t in range(3):
            at = start + PIECE * t
            tile = third[block:, at - at % LANES : at - at % LANES + LANES]
            tail_ref[pl.ds(t, rest, stride=3), :] = pltpu.roll(tile, (WIDTH - at) % LANES, 1)
        piece = third[:block, start : start + WIDTH]
        piece = jnp.concatenate([piece, jnp.zeros((block, PIECE), F32)], axis=1)
        out_ref[block * g : block * (g + 1), :] = jnp.where(lane < WIDTH, piece, tail_ref[...]).astype(BF16)


def arrival_order(owners):
    block = owners * MESSAGE
    comps = owners * COMPS
    table = np.zeros((ROWS * comps, ROWS * comps), np.float32)
    for owner in range(owners):
        for row in range(ROWS):
            for j in range(MAIN):
                table[row * comps + owner * COMPS + j, owner * MESSAGE + row * MAIN + j] = 1
            for i in range(2):
                table[row * comps + owner * COMPS + MAIN + i, block + owner * MAIN + row * 2 + i] = 1
    return table


VMEM = pl.BlockSpec(memory_space=pltpu.VMEM)
HBM = pl.BlockSpec(memory_space=pltpu.HBM)
SPREAD_FLOPS = 2 * 10**10


def per_device(tiles, owners, field, norm_field, vertical, x_filter, y_filter):
    lines, comps, width = field.shape
    total = tiles * owners * MESSAGE
    message_rows = jax.ShapeDtypeStruct((total, LANES), BF16)
    rows_scratch = pltpu.VMEM((total, LANES), F32)
    field_scratch = pltpu.VMEM((comps, width, lines), BF16)
    sems = pltpu.SemaphoreType.DMA

    def call(kernel, name, out_shape, in_specs, out_specs, scratch, *operands, flops):
        return pl.pallas_call(
            kernel,
            out_shape=out_shape,
            in_specs=in_specs,
            out_specs=out_specs,
            scratch_shapes=scratch,
            compiler_params=pltpu.CompilerParams(vmem_limit_bytes=40 * 1024 * 1024),
            cost_estimate=pl.CostEstimate(flops=flops, bytes_accessed=sum(a.nbytes for a in operands), transcendentals=0),
            name=name,
        )(*operands)

    def exchange(rows):
        grouped = rows.reshape(tiles * owners, MESSAGE // 2, 2, LANES)
        moved = lax.all_to_all(grouped, ("gx", "gy"), split_axis=0, concat_axis=0, tiled=True)
        return moved.reshape(total, LANES)

    own = jnp.transpose(field, (1, 2, 0))
    rows = call(spread_kernel, "spread", message_rows, [VMEM, VMEM], VMEM, [rows_scratch], own, y_filter, flops=SPREAD_FLOPS)
    rows = exchange(rows)
    scratch = [rows_scratch, pltpu.VMEM((owners * MESSAGE, LANES), F32)]
    middle = functools.partial(middle_kernel, tiles=tiles, owners=owners)
    order = jnp.asarray(arrival_order(owners), BF16)
    rows = call(middle, "middle", message_rows, [VMEM] * 5, VMEM, scratch, rows, x_filter, norm_field, vertical, order, flops=5 * 10**9)
    rows = exchange(rows)
    result = jax.ShapeDtypeStruct((comps, width, lines), BF16)
    result = call(gather_kernel, "gather", result, [VMEM, VMEM], HBM, [rows_scratch, field_scratch, sems((4,))], rows, y_filter, flops=10**9)
    return jnp.transpose(result, (2, 0, 1))


def solution(mesh):
    return jax.shard_map(
        functools.partial(per_device, mesh.shape["gx"], mesh.shape["gy"]),
        mesh=mesh,
        in_specs=(P(None, "gy", "gx"), P(("gx", "gy"), None, None), P(), P(), P()),
        out_specs=P(None, "gy", "gx"),
        check_vma=False,
    )
```

time: 107 us -> 103 us (0.963)
  Pallas kernels: 11.7 us -> 9.64 us
  local copies, waits for them, and re-layouts: 4.22 us -> 2.56 us
    pallas_call x3, Pallas kernels: 11.7 us -> 9.64 us  [call(): pl.pallas_call(kernel, out_shape=out_shape, in_specs=in_specs, out_specs=...]
    unnamed x14, local copies, waits for them, and re-layouts: 4.22 us -> 2.56 us
where the time goes in v2:
time: 103 us
  blocking collectives  90.4 us (88%)
  Pallas kernels  9.64 us (9%)
  local copies, waits for them, and re-layouts  2.56 us (2%)
    all_to_all x2, blocking collectives, exchange(): lax.all_to_all(grouped, ('gx', 'gy'), split_axis=0, concat_axis=0, tiled=...  90.4 us
    pallas_call x3, Pallas kernels, call(): pl.pallas_call(kernel, out_shape=out_shape, in_specs=in_specs, out_specs=...  9.64 us
    unnamed x14, local copies, waits for them, and re-layouts  2.56 us

profile of v2, /device:TPU:1, one launch (start us, length us, event | category | flops | bytes accessed | tf_op | source)
XLA Modules:
  0.0 102.6 jit_solution(8056132830610363892)
XLA Ops:
  0.0 0.0 copy-start.2
  0.0 1.3 %copy-done.2 = bf16[768,8,96]{0,2,1:T(8,128)(2,1)S(1)} copy-done((bf16[768,8,96]{0,2,1:T(8,128)(2,1)S(1)}, bf16[768,8,96]{0,2,1:T(8,128)(2,1)}, u32[]{:S(2)}) %copy-start.2) | copy-done | bytes 1179672
  1.3 0.0 copy-start.3
  1.3 1.3 %copy-done.3 = bf16[768,768]{1,0:T(8,128)(2,1)S(1)} copy-done((bf16[768,768]{1,0:T(8,128)(2,1)S(1)}, bf16[768,768]{1,0:T(8,128)(2,1)}, u32[]{:S(2)}) %copy-start.3) | copy-done | bytes 1179672
  2.5 0.0 copy-start
  2.5 0.0 copy-start.5
  2.5 0.0 copy-start.6
  2.5 1.2 %spread.1 = bf16[4608,128]{1,0:T(8,128)(2,1)S(1)} custom-call(bf16[8,96,768]{2,1,0:T(8,128)(2,1)S(1)} %bitcast.10, bf16[768,768]{1,0:T(8,128)(2,1)S(1)} %copy-done.3), custom_call_target="tpu_custom_call" | custom-call | flops 20000000000 | bytes 2359296 | tf_op jit(solution)/shard_map/spread/pallas_call | solution.py:143
  3.8 0.0 copy-start.1
  3.8 50.7 %all_to_all.10 = bf16[256,9,2,128]{3,2,1,0:T(2,128)(2,1)S(1)} all-to-all(bf16[256,9,2,128]{3,2,1,0:T(2,128)(2,1)S(1)} %bitcast.9), channel_id=1, replica_groups=mesh['gx'=16,'gy'=16] {'gx','gy'}, dimensions={0} | all-to-all | bytes 2359296 | tf_op jit(solution)/shard_map/all_to_all | solution.py:156
  54.4 0.0 copy-done
  54.4 0.0 copy-done.5
  54.4 0.0 copy-done.6
  54.4 0.0 copy-done.1
  54.5 6.4 %middle.1 = bf16[4608,128]{1,0:T(8,128)(2,1)S(1)} custom-call(bf16[4608,128]{1,0:T(8,128)(2,1)S(1)} %bitcast.6, bf16[1536,1536]{1,0:T(8,128)(2,1)S(1)} %copy-done, f32[3,128,1536]{2,1,0:T(8,128)S(1)} %copy-done.1, f32[2,64,64]{2,1,0:T(8,128)S(1)} %copy-done.5, bf16[384,384]{1,0:T(8,128)(2,1)S(1)} %copy-done.6), custom_call_target="tpu_custom_call" | custom-call | flops 5000000000 | bytes 8585216 | tf_op jit(solution)/shard_map/middle/pallas_call | solution.py:143
  60.8 0.0 copy-start.4
  60.8 39.7 %all_to_all.11 = bf16[256,9,2,128]{3,2,1,0:T(2,128)(2,1)S(1)} all-to-all(bf16[256,9,2,128]{3,2,1,0:T(2,128)(2,1)S(1)} %bitcast.7), channel_id=1, replica_groups=mesh['gx'=16,'gy'=16] {'gx','gy'}, dimensions={0} | all-to-all | bytes 2359296 | tf_op jit(solution)/shard_map/all_to_all | solution.py:156
  100.6 0.0 copy-done.4
  100.6 2.1 %gather.1 = bf16[8,96,768]{2,1,0:T(8,128)(2,1)} custom-call(bf16[4608,128]{1,0:T(8,128)(2,1)S(1)} %bitcast.8, bf16[768,768]{1,0:T(8,128)(2,1)S(1)} %copy-done.4), custom_call_target="tpu_custom_call" | custom-call | flops 1000000000 | bytes 2359296 | tf_op jit(solution)/shard_map/gather/pallas_call | solution.py:143
Async XLA Ops:
  0.0 1.3 %copy-start.2 = (bf16[768,8,96]{0,2,1:T(8,128)(2,1)S(1)}, bf16[768,8,96]{0,2,1:T(8,128)(2,1)}, u32[]{:S(2)}) copy-start(bf16[768,8,96]{0,2,1:T(8,128)(2,1)} %param.6) | copy-start | bytes 3538948
  1.3 1.3 %copy-start.3 = (bf16[768,768]{1,0:T(8,128)(2,1)S(1)}, bf16[768,768]{1,0:T(8,128)(2,1)}, u32[]{:S(2)}) copy-start(bf16[768,768]{1,0:T(8,128)(2,1)} %filter_ref.5) | copy-start | bytes 3538948
  2.5 51.9 %copy-start = (bf16[1536,1536]{1,0:T(8,128)(2,1)S(1)}, bf16[1536,1536]{1,0:T(8,128)(2,1)}, u32[]{:S(2)}) copy-start(bf16[1536,1536]{1,0:T(8,128)(2,1)} %filter_ref.4) | copy-start | bytes 14155780
  2.5 51.9 %copy-start.5 = (f32[2,64,64]{2,1,0:T(8,128)S(1)}, f32[2,64,64]{2,1,0:T(8,128)}, u32[]{:S(2)}) copy-start(f32[2,64,64]{2,1,0:T(8,128)} %vertical_ref.1) | copy-start | bytes 98308
  2.5 51.9 %copy-start.6 = (bf16[384,384]{1,0:T(8,128)(2,1)S(1)}, bf16[384,384]{1,0:T(8,128)(2,1)}, u32[]{:S(2)}) copy-start(bf16[384,384]{1,0:T(8,128)(2,1)} %constant.2.clone.order_ref) | copy-start | bytes 884740
  3.8 50.7 %copy-start.1 = (f32[3,128,1536]{2,1,0:T(8,128)S(1)}, f32[3,128,1536]{2,1,0:T(8,128)}, u32[]{:S(2)}) copy-start(f32[3,128,1536]{2,1,0:T(8,128)} %norm_ref.1) | copy-start | bytes 7077892
  60.8 39.8 %copy-start.4 = (bf16[768,768]{1,0:T(8,128)(2,1)S(1)}, bf16[768,768]{1,0:T(8,128)(2,1)}, u32[]{:S(2)}) copy-start(bf16[768,768]{1,0:T(8,128)(2,1)} %filter_ref.5) | copy-start | bytes 3538948

commit v3 on v2

--- a/solution.py
+++ b/solution.py
@@ -23,7 +23,33 @@
     return lax.dot_general(a, b, ((contract[:1], contract[1:]), ((), ())), preferred_element_type=F32)
 
 
-def spread_kernel(field_ref, filter_ref, out_ref, rows_ref):
+def level_weight(vertical_ref):
+    size = vertical_ref.shape[0] * vertical_ref.shape[1]
+    rows = []
+    for s in range(vertical_ref.shape[0]):
+        factor = vertical_ref[s]
+        weight = lax.dot_general(
+            factor, factor, (((1,), (1,)), ((), ())), precision=lax.Precision.HIGHEST, preferred_element_type=F32
+        )
+        blank = jnp.zeros_like(weight)
+        rows.append(jnp.concatenate([weight if n == s else blank for n in range(size // weight.shape[0])], axis=1))
+    full = jnp.concatenate(rows, axis=0)
+    high = full.astype(BF16)
+    low = (full - high.astype(F32)).astype(BF16)
+    return jnp.concatenate([high, high, low], axis=1)
+
+
+def spread_kernel(
+    field_hbm, filter_hbm, vertical_hbm, out_ref, weight_ref, field_ref, filter_ref, vertical_ref, rows_ref, sems
+):
+    pairs = ((vertical_hbm, vertical_ref), (field_hbm, field_ref), (filter_hbm, filter_ref))
+    loads = [pltpu.make_async_copy(source, target, sems.at[n]) for n, (source, target) in enumerate(pairs)]
+    for load in loads:
+        load.start()
+    loads[0].wait()
+    weight_ref[...] = level_weight(vertical_ref)
+    for load in loads[1:]:
+        load.wait()
     lines = filter_ref.shape[0]
     parts = []
     for j in range(MAIN):
@@ -60,17 +86,8 @@
 
 
 def middle_kernel(
-    rows_in_ref, filter_ref, norm_ref, vertical_ref, order_ref, out_ref, rows_ref, tail_ref, *, tiles, owners
+    rows_in_ref, filter_ref, norm_ref, weight_ref, order_ref, out_ref, rows_ref, tail_ref, *, tiles, owners
 ):
-    weights = []
-    for s in range(vertical_ref.shape[0]):
-        factor = vertical_ref[s]
-        weight = lax.dot_general(
-            factor, factor, (((1,), (1,)), ((), ())), precision=lax.Precision.HIGHEST, preferred_element_type=F32
-        )
-        high = weight.astype(BF16)
-        low = (weight - high.astype(F32)).astype(BF16)
-        weights.append(jnp.concatenate([high, high, low], axis=1))
     filt = filter_ref[...]
     order = order_ref[...]
     block = owners * MESSAGE
@@ -87,23 +104,22 @@
     second = dot(lines, filt, (1, 0)).astype(BF16)
     second = dot(order, second, (1, 0))
     comps = norm_ref.shape[1]
-    levels = vertical_ref.shape[1]
     raised = []
     for r in range(ROWS):
-        for s in range(vertical_ref.shape[0]):
-            span = slice(s * levels, (s + 1) * levels)
-            scales = norm_ref[r, span, :]
-            scaled = scales * second[r * comps + s * levels : r * comps + (s + 1) * levels]
-            upper = scaled.astype(BF16)
-            under = (scaled - upper.astype(F32)).astype(BF16)
-            product = dot(weights[s], jnp.concatenate([upper, under, upper], axis=0), (1, 0))
-            raised.append((scales * product).astype(BF16))
+        scales = norm_ref[r]
+        scaled = scales * second[r * comps : (r + 1) * comps]
+        upper = scaled.astype(BF16)
+        under = (scaled - upper.astype(F32)).astype(BF16)
+        product = dot(weight_ref[...], jnp.concatenate([upper, under, upper], axis=0), (1, 0))
+        raised.append((scales * product).astype(BF16))
     middle = jnp.concatenate(raised, axis=0)
     middle = dot(order, middle, (0, 0)).astype(BF16)
-    third = dot(middle, filt, (1, 1))
     lane = lax.broadcasted_iota(jnp.int32, (block, LANES), 1)
+    half = tiles // 2
     for g in range(tiles):
-        start = WIDTH * g
+        if g % half == 0:
+            third = dot(middle, filt[WIDTH * g : WIDTH * (g + half)], (1, 1))
+        start = WIDTH * (g % half)
         for t in range(3):
             at = start + PIECE * t
             tile = third[block:, at - at % LANES : at - at % LANES + LANES]
@@ -156,13 +172,20 @@
         moved = lax.all_to_all(grouped, ("gx", "gy"), split_axis=0, concat_axis=0, tiled=True)
         return moved.reshape(total, LANES)
 
-    own = jnp.transpose(field, (1, 2, 0))
-    rows = call(spread_kernel, "spread", message_rows, [VMEM, VMEM], VMEM, [rows_scratch], own, y_filter, flops=SPREAD_FLOPS)
+    def in_hbm(array):
+        return pltpu.with_memory_space_constraint(array, pltpu.HBM)
+
+    levels = vertical.shape[0] * vertical.shape[1]
+    weight = jax.ShapeDtypeStruct((levels, 3 * levels), BF16)
+    scratch = [field_scratch] + [pltpu.VMEM(a.shape, a.dtype) for a in (y_filter, vertical)] + [rows_scratch, sems((3,))]
+    operands = [in_hbm(a) for a in (jnp.transpose(field, (1, 2, 0)), y_filter, vertical)]
+    out = (message_rows, weight)
+    rows, weight = call(spread_kernel, "spread", out, [HBM] * 3, (VMEM, VMEM), scratch, *operands, flops=SPREAD_FLOPS)
     rows = exchange(rows)
     scratch = [rows_scratch, pltpu.VMEM((owners * MESSAGE, LANES), F32)]
     middle = functools.partial(middle_kernel, tiles=tiles, owners=owners)
     order = jnp.asarray(arrival_order(owners), BF16)
-    rows = call(middle, "middle", message_rows, [VMEM] * 5, VMEM, scratch, rows, x_filter, norm_field, vertical, order, flops=5 * 10**9)
+    rows = call(middle, "middle", message_rows, [VMEM] * 5, VMEM, scratch, rows, x_filter, norm_field, weight, order, flops=5 * 10**9)
     rows = exchange(rows)
     result = jax.ShapeDtypeStruct((comps, width, lines), BF16)
     result = call(gather_kernel, "gather", result, [VMEM, VMEM], HBM, [rows_scratch, field_scratch, sems((4,))], rows, y_filter, flops=10**9)

time: 103 us -> 102 us (level)
  local copies, waits for them, and re-layouts: 2.56 us -> 0.02 us
  Pallas kernels: 9.64 us -> 11.3 us
    unnamed x14 -> x8, local copies, waits for them, and re-layouts: 2.56 us -> 0.02 us
    pallas_call x3, Pallas kernels: 9.64 us -> 11.3 us  [call(): pl.pallas_call(kernel, out_shape=out_shape, in_specs=in_specs, out_specs=...]
where the time goes in v3:
time: 102 us
  blocking collectives  90.4 us (89%)
  Pallas kernels  11.3 us (11%)
    all_to_all x2, blocking collectives, exchange(): lax.all_to_all(grouped, ('gx', 'gy'), split_axis=0, concat_axis=0, tiled=...  90.4 us
    pallas_call x3, Pallas kernels, call(): pl.pallas_call(kernel, out_shape=out_shape, in_specs=in_specs, out_specs=...  11.3 us

profile of v3, /device:TPU:1, one launch (start us, length us, event | category | flops | bytes accessed | tf_op | source)
XLA Modules:
  0.0 101.7 jit_solution(15801175119774473232)
XLA Ops:
  0.0 0.0 copy-start
  0.0 0.0 copy-start.3
  0.0 3.0 %spread.1 = (bf16[4608,128]{1,0:T(8,128)(2,1)S(1)}, bf16[128,384]{1,0:T(8,128)(2,1)S(1)}) custom-call(bf16[8,96,768]{2,1,0:T(8,128)(2,1)} %bitcast.10, bf16[768,768]{1,0:T(8,128)(2,1)} %filter_ref.3, f32[2,64,64]{2,1,0:T(8,128)} %vertical_hbm.1), custom_call_target="tpu_custom_call" | custom-call | flops 20000000000 | bytes 2392064 | tf_op jit(solution)/shard_map/spread/pallas_call | solution.py:159
  3.1 0.0 copy-start.1
  3.1 50.7 %all_to_all.10 = bf16[256,9,2,128]{3,2,1,0:T(2,128)(2,1)S(1)} all-to-all(bf16[256,9,2,128]{3,2,1,0:T(2,128)(2,1)S(1)} %bitcast.8), channel_id=1, replica_groups=mesh['gx'=16,'gy'=16] {'gx','gy'}, dimensions={0} | all-to-all | bytes 2359296 | tf_op jit(solution)/shard_map/all_to_all | solution.py:172
  53.7 0.0 copy-done
  53.7 0.0 copy-done.3
  53.7 0.0 copy-done.1
  53.7 6.2 %middle.1 = bf16[4608,128]{1,0:T(8,128)(2,1)S(1)} custom-call(bf16[4608,128]{1,0:T(8,128)(2,1)S(1)} %bitcast.6, bf16[1536,1536]{1,0:T(8,128)(2,1)S(1)} %copy-done, f32[3,128,1536]{2,1,0:T(8,128)S(1)} %copy-done.1, bf16[128,384]{1,0:T(8,128)(2,1)S(1)} %get-tuple-element.8.weight_ref, bf16[384,384]{1,0:T(8,128)(2,1)S(1)} %copy-done.3), custom_call_target="tpu_custom_call" | custom-call | flops 5000000000 | bytes 8650752 | tf_op jit(solution)/shard_map/middle/pallas_call | solution.py:159
  59.9 0.0 copy-start.2
  59.9 39.7 %all_to_all.11 = bf16[256,9,2,128]{3,2,1,0:T(2,128)(2,1)S(1)} all-to-all(bf16[256,9,2,128]{3,2,1,0:T(2,128)(2,1)S(1)} %bitcast.7), channel_id=1, replica_groups=mesh['gx'=16,'gy'=16] {'gx','gy'}, dimensions={0} | all-to-all | bytes 2359296 | tf_op jit(solution)/shard_map/all_to_all | solution.py:172
  99.7 0.0 copy-done.2
  99.7 2.1 %gather.1 = bf16[8,96,768]{2,1,0:T(8,128)(2,1)} custom-call(bf16[4608,128]{1,0:T(8,128)(2,1)S(1)} %bitcast.9, bf16[768,768]{1,0:T(8,128)(2,1)S(1)} %copy-done.2), custom_call_target="tpu_custom_call" | custom-call | flops 1000000000 | bytes 2359296 | tf_op jit(solution)/shard_map/gather/pallas_call | solution.py:159
Async XLA Ops:
  0.0 53.7 %copy-start = (bf16[1536,1536]{1,0:T(8,128)(2,1)S(1)}, bf16[1536,1536]{1,0:T(8,128)(2,1)}, u32[]{:S(2)}) copy-start(bf16[1536,1536]{1,0:T(8,128)(2,1)} %filter_ref.2) | copy-start | bytes 14155780
  0.0 53.7 %copy-start.3 = (bf16[384,384]{1,0:T(8,128)(2,1)S(1)}, bf16[384,384]{1,0:T(8,128)(2,1)}, u32[]{:S(2)}) copy-start(bf16[384,384]{1,0:T(8,128)(2,1)} %constant.2.clone.order_ref) | copy-start | bytes 884740
  3.1 50.7 %copy-start.1 = (f32[3,128,1536]{2,1,0:T(8,128)S(1)}, f32[3,128,1536]{2,1,0:T(8,128)}, u32[]{:S(2)}) copy-start(f32[3,128,1536]{2,1,0:T(8,128)} %norm_ref.1) | copy-start | bytes 7077892
  59.9 39.8 %copy-start.2 = (bf16[768,768]{1,0:T(8,128)(2,1)S(1)}, bf16[768,768]{1,0:T(8,128)(2,1)}, u32[]{:S(2)}) copy-start(bf16[768,768]{1,0:T(8,128)(2,1)} %filter_ref.3) | copy-start | bytes 3538948

commit v4 on v3

--- a/solution.py
+++ b/solution.py
@@ -2,7 +2,6 @@
 
 import jax
 import jax.numpy as jnp
-import numpy as np
 from jax import lax
 from jax.experimental import pallas as pl
 from jax.experimental.pallas import tpu as pltpu
@@ -36,6 +35,11 @@
     full = jnp.concatenate(rows, axis=0)
     high = full.astype(BF16)
     low = (full - high.astype(F32)).astype(BF16)
+    owners = size // COMPS
+    row = lax.broadcasted_iota(jnp.int32, (size, size), 0)
+    col = lax.broadcasted_iota(jnp.int32, (size, size), 1)
+    order = (COMPS * (row % owners) + row // owners == col).astype(BF16)
+    high, low = (dot(dot(order, part, (1, 0)).astype(BF16), order, (1, 1)).astype(BF16) for part in (high, low))
     return jnp.concatenate([high, high, low], axis=1)
 
 
@@ -86,60 +90,60 @@
 
 
 def middle_kernel(
-    rows_in_ref, filter_ref, norm_ref, weight_ref, order_ref, out_ref, rows_ref, tail_ref, *, tiles, owners
+    rows_in_ref, filter_ref, norm_ref, weight_ref, out_ref, rows_ref, stage_ref, tiled_ref, *, tiles, owners
 ):
+    blocks = tiled_ref.shape[0]
+    for n in range(blocks):
+        tiled_ref[n] = norm_ref[:, :, LANES * n : LANES * (n + 1)]
+    block = owners * MESSAGE
+    rows_ref[...] = rows_in_ref[...].astype(F32)
+
+    def arrived(g, r, j):
+        return rows_ref[pl.ds(block * g + MAIN * r + j, owners, stride=MESSAGE), :]
+
+    def scales(r):
+        parts = []
+        for c in range(COMPS):
+            pieces = [tiled_ref.at[n, r][pl.ds(c, owners, stride=COMPS), :] for n in range(blocks)]
+            parts.append(jnp.concatenate(pieces, axis=1))
+        return jnp.concatenate(parts, axis=0)
+
+    lines = []
+    for r in range(ROWS):
+        rows = [[arrived(g, r, j) for j in range(MAIN)] for g in range(tiles)]
+        for j in range(MAIN):
+            lines.append(jnp.concatenate([row[j][:, :WIDTH] for row in rows], axis=1).astype(BF16))
+        for i in range(2):
+            pieces = [row[3 * i + t][:, WIDTH:] for row in rows for t in range(3)]
+            lines.append(jnp.concatenate(pieces, axis=1).astype(BF16))
     filt = filter_ref[...]
-    order = order_ref[...]
-    block = owners * MESSAGE
-    rest = block // 3
-    rows_ref[...] = rows_in_ref[...].astype(F32)
-    main = [rows_ref[block * g : block * (g + 1), :WIDTH] for g in range(tiles)]
-    left = jnp.concatenate(main, axis=1).astype(BF16)
-    tail = []
-    for g in range(tiles):
-        for t in range(3):
-            tail.append(rows_ref[pl.ds(block * g + t, rest, stride=3), :][:, WIDTH:])
-    below = jnp.concatenate(tail, axis=1).astype(BF16)
-    lines = jnp.concatenate([left, below], axis=0)
-    second = dot(lines, filt, (1, 0)).astype(BF16)
-    second = dot(order, second, (1, 0))
-    comps = norm_ref.shape[1]
+    second = dot(jnp.concatenate(lines, axis=0), filt, (1, 0)).astype(BF16).astype(F32)
+    comps = owners * COMPS
     raised = []
     for r in range(ROWS):
-        scales = norm_ref[r]
-        scaled = scales * second[r * comps : (r + 1) * comps]
+        scaled = scales(r) * second[r * comps : (r + 1) * comps]
         upper = scaled.astype(BF16)
         under = (scaled - upper.astype(F32)).astype(BF16)
         product = dot(weight_ref[...], jnp.concatenate([upper, under, upper], axis=0), (1, 0))
-        raised.append((scales * product).astype(BF16))
+        raised.append((scales(r) * product).astype(BF16))
     middle = jnp.concatenate(raised, axis=0)
-    middle = dot(order, middle, (0, 0)).astype(BF16)
-    lane = lax.broadcasted_iota(jnp.int32, (block, LANES), 1)
+    lane = lax.broadcasted_iota(jnp.int32, (owners, LANES), 1)
     half = tiles // 2
     for g in range(tiles):
         if g % half == 0:
             third = dot(middle, filt[WIDTH * g : WIDTH * (g + half)], (1, 1))
         start = WIDTH * (g % half)
-        for t in range(3):
-            at = start + PIECE * t
-            tile = third[block:, at - at % LANES : at - at % LANES + LANES]
-            tail_ref[pl.ds(t, rest, stride=3), :] = pltpu.roll(tile, (WIDTH - at) % LANES, 1)
-        piece = third[:block, start : start + WIDTH]
-        piece = jnp.concatenate([piece, jnp.zeros((block, PIECE), F32)], axis=1)
-        out_ref[block * g : block * (g + 1), :] = jnp.where(lane < WIDTH, piece, tail_ref[...]).astype(BF16)
-
-
-def arrival_order(owners):
-    block = owners * MESSAGE
-    comps = owners * COMPS
-    table = np.zeros((ROWS * comps, ROWS * comps), np.float32)
-    for owner in range(owners):
-        for row in range(ROWS):
+        for r in range(ROWS):
             for j in range(MAIN):
-                table[row * comps + owner * COMPS + j, owner * MESSAGE + row * MAIN + j] = 1
-            for i in range(2):
-                table[row * comps + owner * COMPS + MAIN + i, block + owner * MAIN + row * 2 + i] = 1
-    return table
+                line = r * comps + j * owners
+                piece = third[line : line + owners, start : start + WIDTH]
+                piece = jnp.concatenate([piece, jnp.zeros((owners, PIECE), F32)], axis=1)
+                line = r * comps + (MAIN + j // 3) * owners
+                at = start + PIECE * (j % 3)
+                tile = third[line : line + owners, at - at % LANES : at - at % LANES + LANES]
+                tile = pltpu.roll(tile, (WIDTH - at) % LANES, 1)
+                stage_ref[pl.ds(MAIN * r + j, owners, stride=MESSAGE), :] = jnp.where(lane < WIDTH, piece, tile)
+        out_ref[block * g : block * (g + 1), :] = stage_ref[...].astype(BF16)
 
 
 VMEM = pl.BlockSpec(memory_space=pltpu.VMEM)
@@ -182,10 +186,12 @@
     out = (message_rows, weight)
     rows, weight = call(spread_kernel, "spread", out, [HBM] * 3, (VMEM, VMEM), scratch, *operands, flops=SPREAD_FLOPS)
     rows = exchange(rows)
-    scratch = [rows_scratch, pltpu.VMEM((owners * MESSAGE, LANES), F32)]
+    blocks = x_filter.shape[0] // LANES
+    norm_scratch = pltpu.VMEM((blocks, ROWS, levels, LANES), F32)
+    scratch = [rows_scratch, pltpu.VMEM((owners * MESSAGE, LANES), F32), norm_scratch]
     middle = functools.partial(middle_kernel, tiles=tiles, owners=owners)
-    order = jnp.asarray(arrival_order(owners), BF16)
-    rows = call(middle, "middle", message_rows, [VMEM] * 5, VMEM, scratch, rows, x_filter, norm_field, weight, order, flops=5 * 10**9)
+    operands = (rows, x_filter, norm_field, weight)
+    rows = call(middle, "middle", message_rows, [VMEM] * 4, VMEM, scratch, *operands, flops=5 * 10**9)
     rows = exchange(rows)
     result = jax.ShapeDtypeStruct((comps, width, lines), BF16)
     result = call(gather_kernel, "gather", result, [VMEM, VMEM], HBM, [rows_scratch, field_scratch, sems((4,))], rows, y_filter, flops=10**9)

time: 102 us -> 101 us (level)
  no operation moved by 1% of the time
where the time goes in v4:
time: 101 us
  blocking collectives  90.4 us (90%)
  Pallas kernels  10.7 us (11%)
    all_to_all x2, blocking collectives, exchange(): lax.all_to_all(grouped, ('gx', 'gy'), split_axis=0, concat_axis=0, tiled=...  90.4 us
    pallas_call x3, Pallas kernels, call(): pl.pallas_call(kernel, out_shape=out_shape, in_specs=in_specs, out_specs=...  10.7 us

profile of v4, /device:TPU:1, one launch (start us, length us, event | category | flops | bytes accessed | tf_op | source)
XLA Modules:
  0.0 101.2 jit_solution(17733757539639420132)
XLA Ops:
  0.0 0.0 copy-start
  0.0 3.1 %spread.1 = (bf16[4608,128]{1,0:T(8,128)(2,1)S(1)}, bf16[128,384]{1,0:T(8,128)(2,1)S(1)}) custom-call(bf16[8,96,768]{2,1,0:T(8,128)(2,1)} %bitcast.10, bf16[768,768]{1,0:T(8,128)(2,1)} %filter_ref.3, f32[2,64,64]{2,1,0:T(8,128)} %vertical_hbm.1), custom_call_target="tpu_custom_call" | custom-call | flops 20000000000 | bytes 2392064 | tf_op jit(solution)/shard_map/spread/pallas_call | solution.py:163
  3.1 0.0 copy-start.1
  3.1 50.7 %all_to_all.10 = bf16[256,9,2,128]{3,2,1,0:T(2,128)(2,1)S(1)} all-to-all(bf16[256,9,2,128]{3,2,1,0:T(2,128)(2,1)S(1)} %bitcast.7), channel_id=1, replica_groups=mesh['gx'=16,'gy'=16] {'gx','gy'}, dimensions={0} | all-to-all | bytes 2359296 | tf_op jit(solution)/shard_map/all_to_all | solution.py:176
  53.7 0.0 copy-done
  53.8 0.0 copy-done.1
  53.8 5.6 %middle.1 = bf16[4608,128]{1,0:T(8,128)(2,1)S(1)} custom-call(bf16[4608,128]{1,0:T(8,128)(2,1)S(1)} %bitcast.6, bf16[1536,1536]{1,0:T(8,128)(2,1)S(1)} %copy-done, f32[3,128,1536]{2,1,0:T(8,128)S(1)} %copy-done.1, bf16[128,384]{1,0:T(8,128)(2,1)S(1)} %get-tuple-element.8.weight_ref), custom_call_target="tpu_custom_call" | custom-call | flops 5000000000 | bytes 8355840 | tf_op jit(solution)/shard_map/middle/pallas_call | solution.py:163
  59.4 0.0 copy-start.2
  59.4 39.8 %all_to_all.11 = bf16[256,9,2,128]{3,2,1,0:T(2,128)(2,1)S(1)} all-to-all(bf16[256,9,2,128]{3,2,1,0:T(2,128)(2,1)S(1)} %bitcast.8), channel_id=1, replica_groups=mesh['gx'=16,'gy'=16] {'gx','gy'}, dimensions={0} | all-to-all | bytes 2359296 | tf_op jit(solution)/shard_map/all_to_all | solution.py:176
  99.1 0.0 copy-done.2
  99.1 2.1 %gather.1 = bf16[8,96,768]{2,1,0:T(8,128)(2,1)} custom-call(bf16[4608,128]{1,0:T(8,128)(2,1)S(1)} %bitcast.9, bf16[768,768]{1,0:T(8,128)(2,1)S(1)} %copy-done.2), custom_call_target="tpu_custom_call" | custom-call | flops 1000000000 | bytes 2359296 | tf_op jit(solution)/shard_map/gather/pallas_call | solution.py:163
Async XLA Ops:
  0.0 53.8 %copy-start = (bf16[1536,1536]{1,0:T(8,128)(2,1)S(1)}, bf16[1536,1536]{1,0:T(8,128)(2,1)}, u32[]{:S(2)}) copy-start(bf16[1536,1536]{1,0:T(8,128)(2,1)} %filter_ref.2) | copy-start | bytes 14155780
  3.1 50.7 %copy-start.1 = (f32[3,128,1536]{2,1,0:T(8,128)S(1)}, f32[3,128,1536]{2,1,0:T(8,128)}, u32[]{:S(2)}) copy-start(f32[3,128,1536]{2,1,0:T(8,128)} %norm_ref.1) | copy-start | bytes 7077892
  59.4 39.8 %copy-start.2 = (bf16[768,768]{1,0:T(8,128)(2,1)S(1)}, bf16[768,768]{1,0:T(8,128)(2,1)}, u32[]{:S(2)}) copy-start(bf16[768,768]{1,0:T(8,128)(2,1)} %filter_ref.3) | copy-start | bytes 3538948

commit v5 on v4

--- a/solution.py
+++ b/solution.py
@@ -46,13 +46,13 @@
 def spread_kernel(
     field_hbm, filter_hbm, vertical_hbm, out_ref, weight_ref, field_ref, filter_ref, vertical_ref, rows_ref, sems
 ):
-    pairs = ((vertical_hbm, vertical_ref), (field_hbm, field_ref), (filter_hbm, filter_ref))
+    pairs = ((field_hbm, field_ref), (filter_hbm, filter_ref), (vertical_hbm, vertical_ref))
     loads = [pltpu.make_async_copy(source, target, sems.at[n]) for n, (source, target) in enumerate(pairs)]
     for load in loads:
         load.start()
-    loads[0].wait()
+    loads[2].wait()
     weight_ref[...] = level_weight(vertical_ref)
-    for load in loads[1:]:
+    for load in loads[:2]:
         load.wait()
     lines = filter_ref.shape[0]
     parts = []

time: 101 us -> 102 us (level)
  no operation moved by 1% of the time
where the time goes in v5:
time: 102 us
  blocking collectives  90.4 us (89%)
  Pallas kernels  11.2 us (11%)
    all_to_all x2, blocking collectives, exchange(): lax.all_to_all(grouped, ('gx', 'gy'), split_axis=0, concat_axis=0, tiled=...  90.4 us
    pallas_call x3, Pallas kernels, call(): pl.pallas_call(kernel, out_shape=out_shape, in_specs=in_specs, out_specs=...  11.2 us

profile of v5, /device:TPU:1, one launch (start us, length us, event | category | flops | bytes accessed | tf_op | source)
XLA Modules:
  0.0 101.7 jit_solution(8601564470240867476)
XLA Ops:
  0.0 0.0 copy-start
  0.0 3.5 %spread.1 = (bf16[4608,128]{1,0:T(8,128)(2,1)S(1)}, bf16[128,384]{1,0:T(8,128)(2,1)S(1)}) custom-call(bf16[8,96,768]{2,1,0:T(8,128)(2,1)} %bitcast.10, bf16[768,768]{1,0:T(8,128)(2,1)} %filter_ref.3, f32[2,64,64]{2,1,0:T(8,128)} %vertical_hbm.1), custom_call_target="tpu_custom_call" | custom-call | flops 20000000000 | bytes 2392064 | tf_op jit(solution)/shard_map/spread/pallas_call | solution.py:163
  3.6 0.0 copy-start.1
  3.6 50.7 %all_to_all.10 = bf16[256,9,2,128]{3,2,1,0:T(2,128)(2,1)S(1)} all-to-all(bf16[256,9,2,128]{3,2,1,0:T(2,128)(2,1)S(1)} %bitcast.7), channel_id=1, replica_groups=mesh['gx'=16,'gy'=16] {'gx','gy'}, dimensions={0} | all-to-all | bytes 2359296 | tf_op jit(solution)/shard_map/all_to_all | solution.py:176
  54.2 0.0 copy-done
  54.2 0.0 copy-done.1
  54.2 5.6 %middle.1 = bf16[4608,128]{1,0:T(8,128)(2,1)S(1)} custom-call(bf16[4608,128]{1,0:T(8,128)(2,1)S(1)} %bitcast.6, bf16[1536,1536]{1,0:T(8,128)(2,1)S(1)} %copy-done, f32[3,128,1536]{2,1,0:T(8,128)S(1)} %copy-done.1, bf16[128,384]{1,0:T(8,128)(2,1)S(1)} %get-tuple-element.8.weight_ref), custom_call_target="tpu_custom_call" | custom-call | flops 5000000000 | bytes 8355840 | tf_op jit(solution)/shard_map/middle/pallas_call | solution.py:163
  59.8 0.0 copy-start.2
  59.8 39.7 %all_to_all.11 = bf16[256,9,2,128]{3,2,1,0:T(2,128)(2,1)S(1)} all-to-all(bf16[256,9,2,128]{3,2,1,0:T(2,128)(2,1)S(1)} %bitcast.8), channel_id=1, replica_groups=mesh['gx'=16,'gy'=16] {'gx','gy'}, dimensions={0} | all-to-all | bytes 2359296 | tf_op jit(solution)/shard_map/all_to_all | solution.py:176
  99.6 0.0 copy-done.2
  99.6 2.1 %gather.1 = bf16[8,96,768]{2,1,0:T(8,128)(2,1)} custom-call(bf16[4608,128]{1,0:T(8,128)(2,1)S(1)} %bitcast.9, bf16[768,768]{1,0:T(8,128)(2,1)S(1)} %copy-done.2), custom_call_target="tpu_custom_call" | custom-call | flops 1000000000 | bytes 2359296 | tf_op jit(solution)/shard_map/gather/pallas_call | solution.py:163
Async XLA Ops:
  0.0 54.2 %copy-start = (bf16[1536,1536]{1,0:T(8,128)(2,1)S(1)}, bf16[1536,1536]{1,0:T(8,128)(2,1)}, u32[]{:S(2)}) copy-start(bf16[1536,1536]{1,0:T(8,128)(2,1)} %filter_ref.2) | copy-start | bytes 14155780
  3.6 50.7 %copy-start.1 = (f32[3,128,1536]{2,1,0:T(8,128)S(1)}, f32[3,128,1536]{2,1,0:T(8,128)}, u32[]{:S(2)}) copy-start(f32[3,128,1536]{2,1,0:T(8,128)} %norm_ref.1) | copy-start | bytes 7077892
  59.8 39.8 %copy-start.2 = (bf16[768,768]{1,0:T(8,128)(2,1)S(1)}, bf16[768,768]{1,0:T(8,128)(2,1)}, u32[]{:S(2)}) copy-start(bf16[768,768]{1,0:T(8,128)(2,1)} %filter_ref.3) | copy-start | bytes 3538948

commit v6 on v4

--- a/solution.py
+++ b/solution.py
@@ -142,8 +142,8 @@
                 at = start + PIECE * (j % 3)
                 tile = third[line : line + owners, at - at % LANES : at - at % LANES + LANES]
                 tile = pltpu.roll(tile, (WIDTH - at) % LANES, 1)
-                stage_ref[pl.ds(MAIN * r + j, owners, stride=MESSAGE), :] = jnp.where(lane < WIDTH, piece, tile)
-        out_ref[block * g : block * (g + 1), :] = stage_ref[...].astype(BF16)
+                stage_ref.at[g % 2][pl.ds(MAIN * r + j, owners, stride=MESSAGE), :] = jnp.where(lane < WIDTH, piece, tile)
+        out_ref[block * g : block * (g + 1), :] = stage_ref[g % 2].astype(BF16)
 
 
 VMEM = pl.BlockSpec(memory_space=pltpu.VMEM)
@@ -188,7 +188,7 @@
     rows = exchange(rows)
     blocks = x_filter.shape[0] // LANES
     norm_scratch = pltpu.VMEM((blocks, ROWS, levels, LANES), F32)
-    scratch = [rows_scratch, pltpu.VMEM((owners * MESSAGE, LANES), F32), norm_scratch]
+    scratch = [rows_scratch, pltpu.VMEM((2, owners * MESSAGE, LANES), F32), norm_scratch]
     middle = functools.partial(middle_kernel, tiles=tiles, owners=owners)
     operands = (rows, x_filter, norm_field, weight)
     rows = call(middle, "middle", message_rows, [VMEM] * 4, VMEM, scratch, *operands, flops=5 * 10**9)

time: 101 us -> 101 us (level)
  no operation moved by 1% of the time
where the time goes in v6:
time: 101 us
  blocking collectives  90.4 us (90%)
  Pallas kernels  10.6 us (10%)
    all_to_all x2, blocking collectives, exchange(): lax.all_to_all(grouped, ('gx', 'gy'), split_axis=0, concat_axis=0, tiled=...  90.4 us
    pallas_call x3, Pallas kernels, call(): pl.pallas_call(kernel, out_shape=out_shape, in_specs=in_specs, out_specs=...  10.6 us

profile of v6, /device:TPU:1, one launch (start us, length us, event | category | flops | bytes accessed | tf_op | source)
XLA Modules:
  0.0 101.1 jit_solution(11536769071080305545)
XLA Ops:
  0.0 0.0 copy-start
  0.0 3.1 %spread.1 = (bf16[4608,128]{1,0:T(8,128)(2,1)S(1)}, bf16[128,384]{1,0:T(8,128)(2,1)S(1)}) custom-call(bf16[8,96,768]{2,1,0:T(8,128)(2,1)} %bitcast.10, bf16[768,768]{1,0:T(8,128)(2,1)} %filter_ref.3, f32[2,64,64]{2,1,0:T(8,128)} %vertical_hbm.1), custom_call_target="tpu_custom_call" | custom-call | flops 20000000000 | bytes 2392064 | tf_op jit(solution)/shard_map/spread/pallas_call | solution.py:163
  3.1 0.0 copy-start.1
  3.1 50.7 %all_to_all.10 = bf16[256,9,2,128]{3,2,1,0:T(2,128)(2,1)S(1)} all-to-all(bf16[256,9,2,128]{3,2,1,0:T(2,128)(2,1)S(1)} %bitcast.7), channel_id=1, replica_groups=mesh['gx'=16,'gy'=16] {'gx','gy'}, dimensions={0} | all-to-all | bytes 2359296 | tf_op jit(solution)/shard_map/all_to_all | solution.py:176
  53.7 0.0 copy-done
  53.8 0.0 copy-done.1
  53.8 5.5 %middle.1 = bf16[4608,128]{1,0:T(8,128)(2,1)S(1)} custom-call(bf16[4608,128]{1,0:T(8,128)(2,1)S(1)} %bitcast.6, bf16[1536,1536]{1,0:T(8,128)(2,1)S(1)} %copy-done, f32[3,128,1536]{2,1,0:T(8,128)S(1)} %copy-done.1, bf16[128,384]{1,0:T(8,128)(2,1)S(1)} %get-tuple-element.8.weight_ref), custom_call_target="tpu_custom_call" | custom-call | flops 5000000000 | bytes 8355840 | tf_op jit(solution)/shard_map/middle/pallas_call | solution.py:163
  59.3 0.0 copy-start.2
  59.3 39.8 %all_to_all.11 = bf16[256,9,2,128]{3,2,1,0:T(2,128)(2,1)S(1)} all-to-all(bf16[256,9,2,128]{3,2,1,0:T(2,128)(2,1)S(1)} %bitcast.8), channel_id=1, replica_groups=mesh['gx'=16,'gy'=16] {'gx','gy'}, dimensions={0} | all-to-all | bytes 2359296 | tf_op jit(solution)/shard_map/all_to_all | solution.py:176
  99.0 0.0 copy-done.2
  99.1 2.1 %gather.1 = bf16[8,96,768]{2,1,0:T(8,128)(2,1)} custom-call(bf16[4608,128]{1,0:T(8,128)(2,1)S(1)} %bitcast.9, bf16[768,768]{1,0:T(8,128)(2,1)S(1)} %copy-done.2), custom_call_target="tpu_custom_call" | custom-call | flops 1000000000 | bytes 2359296 | tf_op jit(solution)/shard_map/gather/pallas_call | solution.py:163
Async XLA Ops:
  0.0 53.8 %copy-start = (bf16[1536,1536]{1,0:T(8,128)(2,1)S(1)}, bf16[1536,1536]{1,0:T(8,128)(2,1)}, u32[]{:S(2)}) copy-start(bf16[1536,1536]{1,0:T(8,128)(2,1)} %filter_ref.2) | copy-start | bytes 14155780
  3.1 50.7 %copy-start.1 = (f32[3,128,1536]{2,1,0:T(8,128)S(1)}, f32[3,128,1536]{2,1,0:T(8,128)}, u32[]{:S(2)}) copy-start(f32[3,128,1536]{2,1,0:T(8,128)} %norm_ref.1) | copy-start | bytes 7077892
  59.3 39.8 %copy-start.2 = (bf16[768,768]{1,0:T(8,128)(2,1)S(1)}, bf16[768,768]{1,0:T(8,128)(2,1)}, u32[]{:S(2)}) copy-start(bf16[768,768]{1,0:T(8,128)(2,1)} %filter_ref.3) | copy-start | bytes 3538948
